TPU v7x, 32 devices: a whole 2x2x4 slice. The times are simulated.
32 devices in a mesh: slab: 16 (over z, y, core), tm: 2 (over x).
Axes of the slice: x: 2, y: 2, z: 4, core: 2. Of those that a mesh axis runs over, the one named last changes fastest.
Arguments:
- recording: bfloat16 [512, 32768], P('tm', 'slab'), may hold values from -6 to 6
- footprints: bfloat16 [2176, 4096], P(None, 'slab'), may hold values from -0.125 to 0.125
- traces: float32 [512, 4096], P('tm', 'slab'), may hold values from 0 to 2
- live_count: int32 [16], replicated, may hold values from 1 to 256, 3072 in all
Outputs:
- new_traces: float32 [512, 4096], P('tm', 'slab')
- new_footprints: bfloat16 [2176, 4096], P('tm', 'slab')
Inputs may be any that keep to these rules, and one draw needn't show every extreme that they name: Slots 0 .. live_count[s] - 1 of slab s are live; some slab has all 256 live.
All inputs are finite; a program needn't handle non-finite values.
Results may differ from a plain program's by a relative error of at most 0.0034.
Values may be sent and summed in bfloat16 or wider, within the bound.
No kernel may reach another device: no remote copies, remote signals or barrier semaphores. Data moves between devices by JAX's collectives and lax.ppermute only.
A program may use at most 64 MiB of HBM per device.

v0:
```python
import functools

import jax
import jax.numpy as jnp
from jax import lax
from jax.experimental import pallas as pl
from jax.experimental.pallas import tpu as pltpu
from jax.sharding import PartitionSpec as P

GROUP = 128
EARLY = 512
BF = jnp.bfloat16
F32 = jnp.float32
WHOLE = pl.BlockSpec(memory_space=pltpu.VMEM)
LEFT_THERE = pl.BlockSpec(memory_space=pl.ANY)
COPIES = pltpu.SemaphoreType.DMA
shape = jax.ShapeDtypeStruct


def mm(left, right):
    return jnp.dot(left, right, preferred_element_type=F32)


def mm_t(left, right):
    return lax.dot_general(left, right, (((1,), (1,)), ((), ())), preferred_element_type=F32)


def t_mm(left, right):
    return lax.dot_general(left, right, (((0,), (0,)), ((), ())), preferred_element_type=F32)


def halves(wide):
    high = wide.astype(BF)
    return high, (wide - high.astype(F32)).astype(BF)


def living(count, block):
    slots = lax.broadcasted_iota(jnp.int32, block.shape, 1)
    return jnp.where(slots < count, block, jnp.zeros_like(block))


def diagonal(square):
    rows = lax.broadcasted_iota(jnp.int32, square.shape, 0)
    columns = lax.broadcasted_iota(jnp.int32, square.shape, 1)
    return jnp.sum(jnp.where(rows == columns, square, 0.0), axis=0, keepdims=True)


def at_end(axis):
    return lax.axis_index(axis) == lax.axis_size(axis) - 1


def odd_slab():
    return lax.axis_index("slab") % 2 == 1


def call(body, outs, in_specs, out_specs, expected, **more):
    return pl.pallas_call(
        body,
        out_shape=outs,
        in_specs=in_specs,
        out_specs=out_specs,
        compiler_params=pltpu.CompilerParams(vmem_limit_bytes=32 * 1024 * 1024),
        cost_estimate=pl.CostEstimate(
            flops=0, bytes_accessed=int(expected * 3_690_000), transcendentals=0
        ),
        **more,
    )


def copied(source, target, sem):
    copy = pltpu.make_async_copy(source, target, sem)
    copy.start()
    return copy


def first_column(which, voxels, rim):
    return pl.multiple_of(rim + which * (voxels // 2 - rim), 128)


def rim_kernel(voxels, live, movie, foot, start, far, near, count, *rest):
    numbers, head, tail, traces, edge, sems = rest[-6:]
    rim = head.shape[0]
    small = [
        copied(live, numbers, sems.at[0]),
        copied(start, traces, sems.at[1]),
        copied(foot.at[pl.ds(0, rim)], head, sems.at[2]),
        copied(foot.at[pl.ds(voxels, rim)], tail, sems.at[3]),
        copied(movie.at[:, pl.ds(0, rim)], edge, sems.at[4]),
    ]
    large = []
    if len(rest) > 6:
        column = first_column(1 - lax.axis_index("tm"), voxels, rim)
        large = [
            copied(movie.at[:, pl.ds(0, rim)], rest[0].at[:, pl.ds(0, rim)], sems.at[5]),
            copied(movie.at[:, pl.ds(column, EARLY)], rest[0].at[:, pl.ds(rim, EARLY)], sems.at[6]),
        ]
    for copy in small:
        copy.wait()
    alive = numbers[lax.axis_index("slab")]
    count[...] = jnp.full(count.shape, alive, jnp.int32)
    high, low = halves(living(alive, traces[...]))
    ends = jnp.where(at_end("slab"), jnp.zeros_like(tail[...]), tail[...])
    forward = mm_t(high, ends) + mm_t(low, ends)
    backward = edge[...].astype(F32) - (mm_t(high, head[...]) + mm_t(low, head[...]))
    odd = odd_slab()
    near[...] = jnp.where(odd, backward, forward).astype(BF)
    far[...] = jnp.where(odd, forward, backward).astype(BF)
    for copy in large:
        copy.wait()


def drive_kernel(voxels, count, movie, foot, start, plan, scale, cross_high, cross_low, rims, masked):
    rim = foot.shape[0] - voxels
    alive = count[0:1]
    masked[:voxels] = living(alive, foot[:voxels])
    ends = living(alive, foot[voxels:])
    masked[voxels:] = jnp.where(at_end("slab"), jnp.zeros_like(ends), ends)
    rims[:rim] = -masked[:rim]
    rims[rim:] = masked[voxels:]
    drive = mm(movie[...], masked[:voxels])
    gram = t_mm(masked[...], masked[...])
    inverse = 1.0 / (diagonal(gram) + 1e-06)
    scale[...] = jnp.broadcast_to(inverse, scale.shape)
    gram_high, gram_low = halves(gram)
    cross_high[...] = gram_high[:GROUP, GROUP:]
    cross_low[...] = gram_low[:GROUP, GROUP:]
    current = living(alive, start[...])
    high, low = halves(current)
    for at in range(0, current.shape[1], GROUP):
        columns = slice(at, at + GROUP)
        coupled = mm(high[:, at:], gram_high[at:, columns]) + mm(high[:, at:], gram_low[at:, columns])
        coupled = coupled + mm(low[:, at:], gram_high[at:, columns])
        plan[:, columns] = current[:, columns] + (drive[:, columns] - coupled) * inverse[:, columns]


def sweep_kernel(plan, scale, cross_high, cross_low, rims, far, near, traces, rounded):
    odd = odd_slab()
    one, two = near[...], far[...]
    beside = jnp.concatenate([jnp.where(odd, one, two), jnp.where(odd, two, one)], axis=1)
    stepped = plan[...] + mm(beside, rims[...]) * scale[0:1]
    first = jnp.maximum(stepped[:, :GROUP], 0.0)
    high, low = halves(first)
    cross = cross_high[...]
    coupled = mm(high, cross) + mm(high, cross_low[...]) + mm(low, cross)
    second = jnp.maximum(stepped[:, GROUP:] - coupled * scale[0:1, GROUP:], 0.0)
    traces[:, :GROUP] = first
    traces[:, GROUP:] = second
    rounded[:, :GROUP] = first.astype(BF)
    rounded[:, GROUP:] = second.astype(BF)


def own_kernel(voxels, rim, movie, foot, fit, early, total, lead, quad, sent_own, seen_other, late, sem):
    here = lax.axis_index("tm")
    width = voxels // 2
    there = pl.multiple_of(first_column(1 - here, voxels, rim) + EARLY, 128)
    copy = copied(movie.at[:, pl.ds(there, width - EARLY)], late, sem)
    traces = fit[...]
    row = pl.multiple_of(jnp.where(here == 0, voxels, 0), rim)
    edge = foot[pl.ds(row, rim)]
    flat = movie[:, :rim].T.astype(F32)
    sent_own[...] = (jnp.where(here == 0, 0.0, flat) - mm_t(edge, traces)).astype(BF)
    seen_other[...] = jnp.where(here == 0, 0.0, early[:, :rim].T.astype(F32)).astype(BF)
    quad[...] = t_mm(traces, traces)
    lead[...] = jnp.where(here == 0, mm(flat.astype(BF), traces), 0.0)
    total[...] = t_mm(movie[:, pl.ds(first_column(here, voxels, rim), width)], traces)
    copy.wait()


def sent_kernel(voxels, foot, fit, sent_own, seen_other, sent):
    rim, frames = sent_own.shape
    row = pl.multiple_of(jnp.where(lax.axis_index("tm") == 0, voxels, 0), rim)
    sent[:, :frames] = sent_own[...]
    seen = seen_other[...].astype(F32) - mm_t(foot[pl.ds(row, rim)], fit[...])
    sent[:, frames:] = seen.astype(BF)


def settled(foot, row, part, high, low, inverse):
    own = foot[pl.ds(pl.multiple_of(row, 128), part.shape[0])]
    return own.astype(F32) + (part - (mm(own, high) + mm(own, low))) * inverse


def level_kernel(voxels, rim, foot, total, lead, quad, early, fit, scale, high, low, base, waiting):
    here = lax.axis_index("tm")
    fitted = fit[...]
    square = quad[...] + t_mm(fitted, fitted)
    inverse = 1.0 / jnp.maximum(diagonal(square), 1.0)
    scale[...] = jnp.broadcast_to(inverse, scale.shape)
    high[...], low[...] = halves(square)
    row = first_column(here, voxels, rim)
    for at in range(EARLY, voxels // 2, 128):
        waiting[at - EARLY:at - EARLY + 128] = settled(
            foot, row + at, total[at:at + 128], high[...], low[...], inverse
        )
    part = lead[...] + jnp.where(here == 0, t_mm(early[:, :rim], fitted), 0.0)
    base[...] = settled(foot, here * voxels, part, high[...], low[...], inverse)


def early_kernel(voxels, rim, foot, total, early, fit, scale, high, low, traces, out, new_tr, moved, sems):
    here = lax.axis_index("tm")
    written = copied(traces, new_tr, sems.at[0])
    fitted = fit[...]
    row = first_column(here, voxels, rim)
    for at in range(0, EARLY, 128):
        part = total[at:at + 128] + t_mm(early[:, rim + at:rim + at + 128], fitted)
        part = settled(foot, row + at, part, high[...], low[...], scale[0:1])
        moved[at:at + 128] = jnp.maximum(part, 0.0).astype(BF)
    skip = rim // 2

    @pl.when(here == 0)
    def _():
        copied(moved, out.at[pl.ds(rim, EARLY)], sems.at[1]).wait()

    @pl.when(here == 1)
    def _():
        copied(moved.at[pl.ds(skip, EARLY - skip)], out.at[pl.ds(0, EARLY - skip)], sems.at[1]).wait()

    written.wait()


def late_kernel(rim, sofar, waiting, late, fit, scale, out, moved, sem):
    here = lax.axis_index("tm")
    length = waiting.shape[0]
    skip = rim // 2
    fitted = fit[...]
    for at in range(0, length, 128):
        part = waiting[at:at + 128] + t_mm(late[:, at:at + 128], fitted) * scale[0:1]
        moved[at:at + 128] = jnp.maximum(part, 0.0).astype(BF)

    @pl.when(here == 0)
    def _():
        copied(moved.at[pl.ds(0, length - skip)], out.at[pl.ds(rim + EARLY, length - skip)], sem).wait()

    @pl.when(here == 1)
    def _():
        copied(moved, out.at[pl.ds(EARLY - skip, length)], sem).wait()


def edge_kernel(sofar, came, fit_own, fit_other, base, scale, out, moved, sem):
    frames = fit_own.shape[0]
    rim = base.shape[0]
    part = mm(came[:, :frames], fit_own[...]) + mm(came[:, frames:], fit_other[...])
    moved[...] = jnp.maximum(base[...] + part * scale[0:1], 0.0).astype(BF)
    row = pl.multiple_of(lax.axis_index("tm") * (out.shape[0] - rim), 64)
    copied(moved, out.at[pl.ds(row, rim)], sem).wait()


def halved(voxels, rim, foot, recording, early, new_tr, rounded):
    frames = recording.shape[0]
    extended, neurons = foot.shape
    slabs = lax.axis_size("slab")
    width, share = voxels // 2, extended // 2
    across = [(0, 1), (1, 0)]
    came_early = lax.ppermute(early, "tm", across)
    other = lax.ppermute(rounded, "tm", across)
    total, lead, quad, sent_own, seen_other, late = call(
        functools.partial(own_kernel, voxels, rim),
        [
            shape((width, neurons), F32),
            shape((rim, neurons), F32),
            shape((neurons, neurons), F32),
            shape((rim, frames), BF),
            shape((rim, frames), BF),
            shape((frames, width - EARLY), BF),
        ],
        [WHOLE] * 4,
        [WHOLE] * 6,
        0.5,
        scratch_shapes=[COPIES],
    )(recording, foot, rounded, came_early)
    came_late = lax.ppermute(late, "tm", across)
    sent = call(
        functools.partial(sent_kernel, voxels),
        shape((rim, 2 * frames), BF),
        [WHOLE] * 4,
        WHOLE,
        0.2,
    )(foot, other, sent_own, seen_other)
    ahead = [(i * 2, i * 2 + 2) for i in range(slabs - 1)]
    behind = [(i * 2 + 3, i * 2 + 1) for i in range(slabs - 1)]
    came = lax.ppermute(sent, ("slab", "tm"), ahead + behind)
    scale, high, low, base, waiting = call(
        functools.partial(level_kernel, voxels, rim),
        [
            shape((8, neurons), F32),
            shape((neurons, neurons), BF),
            shape((neurons, neurons), BF),
            shape((rim, neurons), F32),
            shape((width - EARLY, neurons), F32),
        ],
        [WHOLE] * 6,
        [WHOLE] * 5,
        0.8,
    )(foot, total, lead, quad, came_early, other)
    sofar, new_tr = call(
        functools.partial(early_kernel, voxels, rim),
        [pltpu.HBM((share, neurons), BF), pltpu.HBM((frames, neurons), F32)],
        [WHOLE] * 8,
        [LEFT_THERE] * 2,
        1.2,
        scratch_shapes=[pltpu.VMEM((EARLY, neurons), BF), COPIES((2,))],
    )(foot, total, came_early, other, scale, high, low, new_tr)
    sofar = call(
        functools.partial(late_kernel, rim),
        pltpu.HBM((share, neurons), BF),
        [LEFT_THERE] + [WHOLE] * 4,
        LEFT_THERE,
        1.0,
        input_output_aliases={0: 0},
        scratch_shapes=[pltpu.VMEM((width - EARLY, neurons), BF), COPIES],
    )(sofar, waiting, came_late, other, scale)
    new_foot = call(
        edge_kernel,
        pltpu.HBM((share, neurons), BF),
        [LEFT_THERE] + [WHOLE] * 5,
        LEFT_THERE,
        0.8,
        input_output_aliases={0: 0},
        scratch_shapes=[pltpu.VMEM((rim, neurons), BF), COPIES],
    )(sofar, came, rounded, other, base, scale)
    return new_tr, new_foot


def spread(voxels, rim, foot, recording, rounded):
    slabs, parts = lax.axis_size("slab"), lax.axis_size("tm")
    extended, neurons = foot.shape
    share = extended // parts
    here = lax.axis_index("tm")
    closing = here == parts - 1
    exact = lax.Precision.HIGHEST
    cut = voxels - (share - rim)
    columns = jnp.concatenate([recording[:, :cut], recording[:, :rim], recording[:, cut:]], 1)
    movie = lax.all_to_all(columns, "tm", split_axis=1, concat_axis=0, tiled=True)
    fit = lax.all_gather(rounded, "tm", axis=0, tiled=True)
    edge = jnp.where(here == 0, foot[voxels:], foot[:rim])
    seen = movie[:, :rim].astype(F32)
    sent = jnp.where(here == 0, 0.0, seen) - mm_t(fit, edge)
    ahead = [(i * parts, (i + 1) * parts) for i in range(slabs - 1)]
    behind = [((i + 2) * parts - 1, (i + 1) * parts - 1) for i in range(slabs - 1)]
    lead = jnp.where(closing, 0.0, seen) + lax.ppermute(sent, ("slab", "tm"), ahead + behind)
    lead = lax.dot_general(lead, fit.astype(F32), (((0,), (0,)), ((), ())), precision=exact)
    inner = t_mm(movie[:, rim:], fit)
    total = jnp.where(
        closing, jnp.concatenate([inner, lead], 0), jnp.concatenate([lead, inner], 0)
    )
    square = t_mm(fit, fit)
    own = lax.dynamic_slice_in_dim(foot, here * share, share, 0).astype(F32)
    total = total - jnp.dot(own, square, precision=exact)
    return jnp.maximum(own + total / jnp.maximum(jnp.diagonal(square), 1.0), 0.0).astype(BF)


def on_device(recording, footprints, traces, live_count):
    slabs, parts = lax.axis_size("slab"), lax.axis_size("tm")
    frames, voxels = recording.shape
    extended, neurons = footprints.shape
    rim = extended - voxels
    early_shape = [pltpu.VMEM((frames, rim + EARLY), BF)] if parts == 2 else []
    pinned = [
        pltpu.with_memory_space_constraint(x, pltpu.HBM)
        for x in (live_count, recording, footprints, traces)
    ]
    far, near, count, *early = call(
        functools.partial(rim_kernel, voxels),
        [
            pltpu.VMEM((frames, rim), BF),
            pltpu.VMEM((frames, rim), BF),
            pltpu.VMEM((8, neurons), jnp.int32),
        ]
        + early_shape,
        [LEFT_THERE] * 4,
        [WHOLE] * (3 + len(early_shape)),
        1.5,
        scratch_shapes=[
            pltpu.SMEM(live_count.shape, jnp.int32),
            pltpu.VMEM((rim, neurons), BF),
            pltpu.VMEM((rim, neurons), BF),
            pltpu.VMEM((frames, neurons), F32),
            pltpu.VMEM((frames, rim), BF),
            COPIES((7,)),
        ],
    )(*pinned)
    def swapped(block, first):
        route = [(i, i + 1) for i in range(first, slabs - 1, 2)]
        return lax.ppermute(block, "slab", route + [(j, i) for i, j in route])

    far = swapped(far, 1)
    near = swapped(near, 0)
    plan, scale, cross_high, cross_low, rims, masked = call(
        functools.partial(drive_kernel, voxels),
        [
            shape((frames, neurons), F32),
            shape((8, neurons), F32),
            shape((GROUP, GROUP), BF),
            shape((GROUP, GROUP), BF),
            shape((2 * rim, neurons), BF),
            pltpu.VMEM((extended, neurons), BF),
        ],
        [WHOLE] * 4,
        [WHOLE] * 6,
        1.2,
    )(count, recording, footprints, traces)

    new_tr, rounded = call(
        sweep_kernel,
        [pltpu.VMEM((frames, neurons), F32), pltpu.VMEM((frames, neurons), BF)],
        [WHOLE] * 7,
        [WHOLE, WHOLE],
        0.4,
    )(plan, scale, cross_high, cross_low, rims, far, near)

    if parts == 2:
        return halved(voxels, rim, masked, recording, early[0], new_tr, rounded)
    return new_tr, spread(voxels, rim, masked, recording, rounded)


def solution(mesh):
    placed = (P("tm", "slab"), P(None, "slab"), P("tm", "slab"), P())
    return jax.shard_map(
        on_device,
        mesh=mesh,
        in_specs=placed,
        out_specs=(P("tm", "slab"), P("tm", "slab")),
        check_vma=False,
    )
```

profile of v0, /device:TPU:24, one launch (start us, length us, event | category | flops | bytes accessed | tf_op | source)
XLA Modules:
  0.0 25.3 jit_solution(16248162493870776790)
XLA Ops:
  0.6 0.0 copy-start
  0.6 0.0 copy-start.2
  0.7 0.0 copy-start.1
  0.7 1.5 %shard_map.59 = (bf16[256,128]{1,0:T(8,128)(2,1)S(1)}, bf16[256,128]{1,0:T(8,128)(2,1)S(1)}, s32[8,256]{1,0:T(8,128)S(1)}, bf16[256,640]{1,0:T(8,128)(2,1)S(1)}) custom-call(s32[16]{0:T(128)} %live.1, bf16[256,2048]{1,0:T(8,128)(2,1)} %movie.5, bf16[2176,256]{1,0:T(8,128)(2,1)} %foot.3, f32[256,256]{1,0:T(8,128)} %start.3), custom_call_target="tpu_custom_call" | custom-call | bytes 5535000 | tf_op jit(solution)/shard_map/pallas_call | solution.py:361
  2.2 1.6 %collective-permute-start.2 = (bf16[256,640]{1,0:T(8,128)(2,1)S(1)}, bf16[256,640]{1,0:T(8,128)(2,1)S(1)}, u32[]{:S(2)}, u32[]{:S(2)}) collective-permute-start(bf16[256,640]{1,0:T(8,128)(2,1)S(1)} %get-tuple-element.37), channel_id=1, source_target_pairs={{0,1},{1,0},{2,3},{3,2},{4,5},{5,4},{6,7},{7,6},{8,9},{9,8},{10,11... | collective-permute-start | bytes 983048 | tf_op jit(solution)/shard_map/ppermute | solution.py:253
  3.7 2.5 %collective-permute-start = (bf16[256,128]{1,0:T(8,128)(2,1)S(1)}, bf16[256,128]{1,0:T(8,128)(2,1)S(1)}, u32[]{:S(2)}, u32[]{:S(2)}) collective-permute-start(bf16[256,128]{1,0:T(8,128)(2,1)S(1)} %get-tuple-element.34), channel_id=1, source_target_pairs={{2,4},{6,8},{10,12},{14,16},{18,20},{22,24},{26,28},{4,2},{8,6},{1... | collective-permute-start | bytes 196616 | tf_op jit(solution)/shard_map/ppermute | solution.py:383
  6.2 1.1 %collective-permute-start.1 = (bf16[256,128]{1,0:T(8,128)(2,1)S(1)}, bf16[256,128]{1,0:T(8,128)(2,1)S(1)}, u32[]{:S(2)}, u32[]{:S(2)}) collective-permute-start(bf16[256,128]{1,0:T(8,128)(2,1)S(1)} %get-tuple-element.35), channel_id=1, source_target_pairs={{0,2},{4,6},{8,10},{12,14},{16,18},{20,22},{24,26},{28,30},{2,0},{... | collective-permute-start | bytes 196616 | tf_op jit(solution)/shard_map/ppermute | solution.py:383
  7.3 0.0 copy-done
  7.3 0.0 copy-done.2
  7.3 0.0 copy-done.1
  7.3 1.2 %shard_map.60 = (f32[256,256]{1,0:T(8,128)S(1)}, f32[8,256]{1,0:T(8,128)S(1)}, bf16[128,128]{1,0:T(8,128)(2,1)S(1)}, bf16[128,128]{1,0:T(8,128)(2,1)S(1)}, bf16[...) custom-call(s32[8,256]{1,0:T(8,128)S(1)} %get-tuple-element.27.count, bf16[256,2048]{1,0:T(8,128)(2,1)S(1)} %copy-done, ...), custom_call_target="tpu_custom_call" | custom-call | bytes 4428000 | tf_op jit(solution)/shard_map/pallas_call | solution.py:387
  8.6 1.6 %collective-permute-done.far = bf16[256,128]{1,0:T(8,128)(2,1)S(1)} collective-permute-done((bf16[256,128]{1,0:T(8,128)(2,1)S(1)}, bf16[256,128]{1,0:T(8,128)(2,1)S(1)}, u32[]{:S(2)}, u32[]{:S(2)}) %collective-permute-start) | collective-permute-done | bytes 65568 | tf_op jit(solution)/shard_map/ppermute | solution.py:383
  10.2 0.0 collective-permute-done.1.near
  10.2 0.4 %shard_map.61 = (f32[256,256]{1,0:T(8,128)S(1)}, bf16[256,256]{1,0:T(8,128)(2,1)S(1)}) custom-call(f32[256,256]{1,0:T(8,128)S(1)} %get-tuple-element.29.plan, f32[8,256]{1,0:T(8,128)S(1)} %get-tuple-element.30.scale, bf16[128,128]{1,0:T(8,128)(2,1)S(1)} %get-tuple-element.31.cross_high, bf16[128,128]{1,0:T(8,128)(2,1)S(1)} %get-tuple-element.32.cross_low, ...), custom_call_target="tpu_custom_call" | custom-call | bytes 1476000 | tf_op jit(solution)/shard_map/pallas_call | solution.py:402
  10.6 0.6 %collective-permute-start.3 = (bf16[256,256]{1,0:T(8,128)(2,1)S(1)}, bf16[256,256]{1,0:T(8,128)(2,1)S(1)}, u32[]{:S(2)}, u32[]{:S(2)}) collective-permute-start(bf16[256,256]{1,0:T(8,128)(2,1)S(1)} %get-tuple-element.36.fit.fit_own), channel_id=1, source_target_pairs={{0,1},{1,0},{2,3},{3,2},{4,5},{5,4},{6,7},{7,6},{8,9},{9,8},{10,11... | collective-permute-start | bytes 393224 | tf_op jit(solution)/shard_map/ppermute | solution.py:254
  11.2 0.5 %collective-permute-done.2.early = bf16[256,640]{1,0:T(8,128)(2,1)S(1)} collective-permute-done((bf16[256,640]{1,0:T(8,128)(2,1)S(1)}, bf16[256,640]{1,0:T(8,128)(2,1)S(1)}, u32[]{:S(2)}, u32[]{:S(2)}) %collective-permute-start.2) | collective-permute-done | bytes 327712 | tf_op jit(solution)/shard_map/ppermute | solution.py:253
  11.7 0.4 %shard_map.62 = (f32[1024,256]{1,0:T(8,128)S(1)}, f32[128,256]{1,0:T(8,128)S(1)}, f32[256,256]{1,0:T(8,128)S(1)}, bf16[128,256]{1,0:T(8,128)(2,1)S(1)}, bf16[128...) custom-call(bf16[256,2048]{1,0:T(8,128)(2,1)S(1)} %copy-done, bf16[2176,256]{1,0:T(8,128)(2,1)S(1)} %get-tuple-element.28.foot, ...), custom_call_target="tpu_custom_call" | custom-call | bytes 1845000 | tf_op jit(solution)/shard_map/pallas_call | solution.py:255
  12.1 1.5 %collective-permute-start.4 = (bf16[256,512]{1,0:T(8,128)(2,1)S(1)}, bf16[256,512]{1,0:T(8,128)(2,1)S(1)}, u32[]{:S(2)}, u32[]{:S(2)}) collective-permute-start(bf16[256,512]{1,0:T(8,128)(2,1)S(1)} %get-tuple-element.48), channel_id=1, source_target_pairs={{0,1},{1,0},{2,3},{3,2},{4,5},{5,4},{6,7},{7,6},{8,9},{9,8},{10,11... | collective-permute-start | bytes 786440 | tf_op jit(solution)/shard_map/ppermute | solution.py:270
  13.7 3.4 %collective-permute-done.3.fit.fit_other = bf16[256,256]{1,0:T(8,128)(2,1)S(1)} collective-permute-done((bf16[256,256]{1,0:T(8,128)(2,1)S(1)}, bf16[256,256]{1,0:T(8,128)(2,1)S(1)}, u32[]{:S(2)}, u32[]{:S(2)}) %collective-permute-start.3) | collective-permute-done | bytes 131104 | tf_op jit(solution)/shard_map/ppermute | solution.py:254
  17.1 0.2 shard_map.66
  17.3 1.9 %collective-permute-start.5 = (bf16[128,512]{1,0:T(8,128)(2,1)S(1)}, bf16[128,512]{1,0:T(8,128)(2,1)S(1)}, u32[]{:S(2)}, u32[]{:S(2)}) collective-permute-start(bf16[128,512]{1,0:T(8,128)(2,1)S(1)} %shard_map.66), channel_id=1, source_target_pairs={{0,2},{2,4},{4,6},{6,8},{8,10},{10,12},{12,14},{14,16},{16,18},{18... | collective-permute-start | bytes 393224 | tf_op jit(solution)/shard_map/ppermute | solution.py:280
  19.2 0.6 %shard_map.63 = (f32[8,256]{1,0:T(8,128)S(1)}, bf16[256,256]{1,0:T(8,128)(2,1)S(1)}, bf16[256,256]{1,0:T(8,128)(2,1)S(1)}, f32[128,256]{1,0:T(8,128)S(1)}, f32[512,256]{1,0:T(8,128)S(1)}) custom-call(bf16[2176,256]{1,0:T(8,128)(2,1)S(1)} %get-tuple-element.28.foot, f32[1024,256]{1,0:T(8,128)S(1)} %get-tuple-element.38.total, ...), custom_call_target="tpu_custom_call" | custom-call | bytes 2952000 | tf_op jit(solution)/shard_map/pallas_call | solution.py:281
  19.9 1.2 %shard_map.64 = (bf16[1088,256]{1,0:T(8,128)(2,1)}, f32[256,256]{1,0:T(8,128)}) custom-call(bf16[2176,256]{1,0:T(8,128)(2,1)S(1)} %get-tuple-element.28.foot, f32[1024,256]{1,0:T(8,128)S(1)} %get-tuple-element.38.total, bf16[256,640]{1,0:T(8,128)(2,1)S(1)} %collective-permute-done.2.early, bf16[256,256]{1,0:T(8,128)(2,1)S(1)} %collective-permute-done.3.fit.fit_other, ...), custom_call_target="tpu_custom_call" | custom-call | bytes 4428000 | tf_op jit(solution)/shard_map/pallas_call | solution.py:294
  21.1 0.0 collective-permute-done.4.late
  21.1 1.0 %shard_map.65.sofar = bf16[1088,256]{1,0:T(8,128)(2,1)} custom-call(bf16[1088,256]{1,0:T(8,128)(2,1)} %get-tuple-element.46.sofar, f32[512,256]{1,0:T(8,128)S(1)} %get-tuple-element.47.waiting, bf16[256,512]{1,0:T(8,128)(2,1)S(1)} %collective-permute-done.4.late, ...), custom_call_target="tpu_custom_call", output_to_operand_aliasing={{}: (0, {})} | custom-call | bytes 3690000 | tf_op jit(solution)/shard_map/pallas_call | solution.py:302
  22.1 2.5 %collective-permute-done.5.came = bf16[128,512]{1,0:T(8,128)(2,1)S(1)} collective-permute-done((bf16[128,512]{1,0:T(8,128)(2,1)S(1)}, bf16[128,512]{1,0:T(8,128)(2,1)S(1)}, u32[]{:S(2)}, u32[]{:S(2)}) %collective-permute-start.5) | collective-permute-done | bytes 131104 | tf_op jit(solution)/shard_map/ppermute | solution.py:280
  24.5 0.8 %shard_map.67 = bf16[1088,256]{1,0:T(8,128)(2,1)} custom-call(bf16[1088,256]{1,0:T(8,128)(2,1)} %shard_map.65.sofar, bf16[128,512]{1,0:T(8,128)(2,1)S(1)} %collective-permute-done.5.came, bf16[256,256]{1,0:T(8,128)(2,1)S(1)} %get-tuple-element.36.fit.fit_own, ...), custom_call_target="tpu_custom_call", output_to_operand_aliasing={{}: (0, {})} | custom-call | bytes 2952000 | tf_op jit(solution)/shard_map/pallas_call | solution.py:311
Async XLA Ops:
  0.6 6.7 %copy-start = (bf16[256,2048]{1,0:T(8,128)(2,1)S(1)}, bf16[256,2048]{1,0:T(8,128)(2,1)}, u32[]{:S(2)}) copy-start(bf16[256,2048]{1,0:T(8,128)(2,1)} %movie.5) | copy-start | bytes 3145732
  0.6 6.7 %copy-start.2 = (f32[256,256]{1,0:T(8,128)S(1)}, f32[256,256]{1,0:T(8,128)}, u32[]{:S(2)}) copy-start(f32[256,256]{1,0:T(8,128)} %start.3) | copy-start | bytes 786436
  0.7 6.7 %copy-start.1 = (bf16[2176,256]{1,0:T(8,128)(2,1)S(1)}, bf16[2176,256]{1,0:T(8,128)(2,1)}, u32[]{:S(2)}) copy-start(bf16[2176,256]{1,0:T(8,128)(2,1)} %foot.3) | copy-start | bytes 3342340
  2.2 9.5 %collective-permute-start.2 = (bf16[256,640]{1,0:T(8,128)(2,1)S(1)}, bf16[256,640]{1,0:T(8,128)(2,1)S(1)}, u32[]{:S(2)}, u32[]{:S(2)}) collective-permute-start(bf16[256,640]{1,0:T(8,128)(2,1)S(1)} %get-tuple-element.37), channel_id=1, source_target_pairs={{0,1},{1,0},{2,3},{3,2},{4,5},{5,4},{6,7},{7,6},{8,9},{9,8},{10,11... | collective-permute-start | bytes 983048 | tf_op jit(solution)/shard_map/ppermute | solution.py:253
  3.7 6.5 %collective-permute-start = (bf16[256,128]{1,0:T(8,128)(2,1)S(1)}, bf16[256,128]{1,0:T(8,128)(2,1)S(1)}, u32[]{:S(2)}, u32[]{:S(2)}) collective-permute-start(bf16[256,128]{1,0:T(8,128)(2,1)S(1)} %get-tuple-element.34), channel_id=1, source_target_pairs={{2,4},{6,8},{10,12},{14,16},{18,20},{22,24},{26,28},{4,2},{8,6},{1... | collective-permute-start | bytes 196616 | tf_op jit(solution)/shard_map/ppermute | solution.py:383
  6.2 4.0 %collective-permute-start.1 = (bf16[256,128]{1,0:T(8,128)(2,1)S(1)}, bf16[256,128]{1,0:T(8,128)(2,1)S(1)}, u32[]{:S(2)}, u32[]{:S(2)}) collective-permute-start(bf16[256,128]{1,0:T(8,128)(2,1)S(1)} %get-tuple-element.35), channel_id=1, source_target_pairs={{0,2},{4,6},{8,10},{12,14},{16,18},{20,22},{24,26},{28,30},{2,0},{... | collective-permute-start | bytes 196616 | tf_op jit(solution)/shard_map/ppermute | solution.py:383
  10.6 6.5 %collective-permute-start.3 = (bf16[256,256]{1,0:T(8,128)(2,1)S(1)}, bf16[256,256]{1,0:T(8,128)(2,1)S(1)}, u32[]{:S(2)}, u32[]{:S(2)}) collective-permute-start(bf16[256,256]{1,0:T(8,128)(2,1)S(1)} %get-tuple-element.36.fit.fit_own), channel_id=1, source_target_pairs={{0,1},{1,0},{2,3},{3,2},{4,5},{5,4},{6,7},{7,6},{8,9},{9,8},{10,11... | collective-permute-start | bytes 393224 | tf_op jit(solution)/shard_map/ppermute | solution.py:254
  12.1 8.9 %collective-permute-start.4 = (bf16[256,512]{1,0:T(8,128)(2,1)S(1)}, bf16[256,512]{1,0:T(8,128)(2,1)S(1)}, u32[]{:S(2)}, u32[]{:S(2)}) collective-permute-start(bf16[256,512]{1,0:T(8,128)(2,1)S(1)} %get-tuple-element.48), channel_id=1, source_target_pairs={{0,1},{1,0},{2,3},{3,2},{4,5},{5,4},{6,7},{7,6},{8,9},{9,8},{10,11... | collective-permute-start | bytes 786440 | tf_op jit(solution)/shard_map/ppermute | solution.py:270
  17.3 7.2 %collective-permute-start.5 = (bf16[128,512]{1,0:T(8,128)(2,1)S(1)}, bf16[128,512]{1,0:T(8,128)(2,1)S(1)}, u32[]{:S(2)}, u32[]{:S(2)}) collective-permute-start(bf16[128,512]{1,0:T(8,128)(2,1)S(1)} %shard_map.66), channel_id=1, source_target_pairs={{0,2},{2,4},{4,6},{6,8},{8,10},{10,12},{12,14},{14,16},{16,18},{18... | collective-permute-start | bytes 393224 | tf_op jit(solution)/shard_map/ppermute | solution.py:280
where the time goes:
time: 25.5 us; the launch traced here: 25.3 us
  starting transfers between devices  9.22 us (36%)
  waiting for transfers between devices  7.99 us (31%)
  Pallas kernels  7.38 us (29%)
  between operations  0.74 us (3%)
    ppermute x2, starting transfers between devices, swapped(): return lax.ppermute(block, 'slab', route + [(j, i) for i, j in route])  3.6 us
    ppermute x1, waiting for transfers between devices, halved(): other = lax.ppermute(rounded, 'tm', across)  3.43 us
    ppermute x1, waiting for transfers between devices, halved(): came = lax.ppermute(sent, ('slab', 'tm'), ahead + behind)  2.45 us
    ppermute x1, starting transfers between devices, halved(): came = lax.ppermute(sent, ('slab', 'tm'), ahead + behind)  1.92 us
    ppermute x2, waiting for transfers between devices, swapped(): return lax.ppermute(block, 'slab', route + [(j, i) for i, j in route])  1.63 us
    ppermute x1, starting transfers between devices, halved(): came_early = lax.ppermute(early, 'tm', across)  1.56 us
    ppermute x1, starting transfers between devices, halved(): came_late = lax.ppermute(late, 'tm', across)  1.55 us
    pallas_call x1, Pallas kernels, on_device(): call(functools.partial(rim_kernel, voxels), [pltpu.VMEM((frames, rim), BF...  1.51 us
  transfers between devices with their start and end apart: 6, of which 4 were waited for; matrix products, arithmetic and copies ran while one was open for 0% of the time, Pallas kernels for 20%

commit v1 on v0

--- a/solution.py
+++ b/solution.py
@@ -267,6 +267,7 @@
         0.5,
         scratch_shapes=[COPIES],
     )(recording, foot, rounded, came_early)
+    late, other = lax.optimization_barrier((late, other))
     came_late = lax.ppermute(late, "tm", across)
     sent = call(
         functools.partial(sent_kernel, voxels),

time: 25.5 us -> 27.1 us (1.063)
  the two profiles are of different devices: /device:TPU:24 before, /device:TPU:0 now
where the time goes in v1:
time: 27.1 us; the launch traced here: 26.9 us
  starting transfers between devices  9.54 us (35%)
  waiting for transfers between devices  9.24 us (34%)
  Pallas kernels  7.37 us (27%)
  between operations  0.76 us (3%)
    ppermute x1, waiting for transfers between devices, halved(): came_late = lax.ppermute(late, 'tm', across)  3.9 us
    ppermute x2, starting transfers between devices, swapped(): return lax.ppermute(block, 'slab', route + [(j, i) for i, j in route])  3.6 us
    ppermute x1, waiting for transfers between devices, halved(): other = lax.ppermute(rounded, 'tm', across)  3.5 us
    ppermute x1, starting transfers between devices, halved(): came_early = lax.ppermute(early, 'tm', across)  3 us
    ppermute x1, waiting for transfers between devices, halved(): came_early = lax.ppermute(early, 'tm', across)  1.83 us
    ppermute x1, starting transfers between devices, halved(): came = lax.ppermute(sent, ('slab', 'tm'), ahead + behind)  1.74 us
    pallas_call x1, Pallas kernels, on_device(): call(functools.partial(rim_kernel, voxels), [pltpu.VMEM((frames, rim), BF...  1.51 us
    pallas_call x1, Pallas kernels, on_device(): call(functools.partial(drive_kernel, voxels), [shape((frames, neurons), F...  1.22 us
  transfers between devices with their start and end apart: 6, of which 3 were waited for; matrix products, arithmetic and copies ran while one was open for 0% of the time, Pallas kernels for 19%

profile of v1, /device:TPU:0, one launch (start us, length us, event | category | flops | bytes accessed | tf_op | source)
XLA Modules:
  0.0 26.9 jit_solution(1702594378251037655)
XLA Ops:
  0.6 0.0 copy-start
  0.6 0.0 copy-start.2
  0.7 0.0 copy-start.1
  0.7 1.5 %shard_map.59 = (bf16[256,128]{1,0:T(8,128)(2,1)S(1)}, bf16[256,128]{1,0:T(8,128)(2,1)S(1)}, s32[8,256]{1,0:T(8,128)S(1)}, bf16[256,640]{1,0:T(8,128)(2,1)S(1)}) custom-call(s32[16]{0:T(128)} %live.1, bf16[256,2048]{1,0:T(8,128)(2,1)} %movie.5, bf16[2176,256]{1,0:T(8,128)(2,1)} %foot.3, f32[256,256]{1,0:T(8,128)} %start.3), custom_call_target="tpu_custom_call" | custom-call | bytes 5535000 | tf_op jit(solution)/shard_map/pallas_call | solution.py:362
  2.2 3.0 %collective-permute-start.2 = (bf16[256,640]{1,0:T(8,128)(2,1)S(1)}, bf16[256,640]{1,0:T(8,128)(2,1)S(1)}, u32[]{:S(2)}, u32[]{:S(2)}) collective-permute-start(bf16[256,640]{1,0:T(8,128)(2,1)S(1)} %get-tuple-element.39), channel_id=1, source_target_pairs={{0,1},{1,0},{2,3},{3,2},{4,5},{5,4},{6,7},{7,6},{8,9},{9,8},{10,11... | collective-permute-start | bytes 983048 | tf_op jit(solution)/shard_map/ppermute | solution.py:253
  5.2 0.7 %collective-permute-start = (bf16[256,128]{1,0:T(8,128)(2,1)S(1)}, bf16[256,128]{1,0:T(8,128)(2,1)S(1)}, u32[]{:S(2)}, u32[]{:S(2)}) collective-permute-start(bf16[256,128]{1,0:T(8,128)(2,1)S(1)} %get-tuple-element.36), channel_id=1, source_target_pairs={{2,4},{6,8},{10,12},{14,16},{18,20},{22,24},{26,28},{4,2},{8,6},{1... | collective-permute-start | bytes 196616 | tf_op jit(solution)/shard_map/ppermute | solution.py:384
  5.8 2.9 %collective-permute-start.1 = (bf16[256,128]{1,0:T(8,128)(2,1)S(1)}, bf16[256,128]{1,0:T(8,128)(2,1)S(1)}, u32[]{:S(2)}, u32[]{:S(2)}) collective-permute-start(bf16[256,128]{1,0:T(8,128)(2,1)S(1)} %get-tuple-element.37), channel_id=1, source_target_pairs={{0,2},{4,6},{8,10},{12,14},{16,18},{20,22},{24,26},{28,30},{2,0},{... | collective-permute-start | bytes 196616 | tf_op jit(solution)/shard_map/ppermute | solution.py:384
  8.8 0.0 copy-done
  8.8 0.0 copy-done.2
  8.8 0.0 copy-done.1
  8.8 1.2 %shard_map.60 = (f32[256,256]{1,0:T(8,128)S(1)}, f32[8,256]{1,0:T(8,128)S(1)}, bf16[128,128]{1,0:T(8,128)(2,1)S(1)}, bf16[128,128]{1,0:T(8,128)(2,1)S(1)}, bf16[...) custom-call(s32[8,256]{1,0:T(8,128)S(1)} %get-tuple-element.29.count, bf16[256,2048]{1,0:T(8,128)(2,1)S(1)} %copy-done, ...), custom_call_target="tpu_custom_call" | custom-call | bytes 4428000 | tf_op jit(solution)/shard_map/pallas_call | solution.py:388
  10.0 0.0 collective-permute-done.far
  10.0 0.0 collective-permute-done.1.near
  10.0 0.4 %shard_map.61 = (f32[256,256]{1,0:T(8,128)S(1)}, bf16[256,256]{1,0:T(8,128)(2,1)S(1)}) custom-call(f32[256,256]{1,0:T(8,128)S(1)} %get-tuple-element.31.plan, f32[8,256]{1,0:T(8,128)S(1)} %get-tuple-element.32.scale, bf16[128,128]{1,0:T(8,128)(2,1)S(1)} %get-tuple-element.33.cross_high, bf16[128,128]{1,0:T(8,128)(2,1)S(1)} %get-tuple-element.34.cross_low, ...), custom_call_target="tpu_custom_call" | custom-call | bytes 1476000 | tf_op jit(solution)/shard_map/pallas_call | solution.py:403
  10.5 0.6 %collective-permute-start.3 = (bf16[256,256]{1,0:T(8,128)(2,1)S(1)}, bf16[256,256]{1,0:T(8,128)(2,1)S(1)}, u32[]{:S(2)}, u32[]{:S(2)}) collective-permute-start(bf16[256,256]{1,0:T(8,128)(2,1)S(1)} %get-tuple-element.38.fit.fit_own), channel_id=1, source_target_pairs={{0,1},{1,0},{2,3},{3,2},{4,5},{5,4},{6,7},{7,6},{8,9},{9,8},{10,11... | collective-permute-start | bytes 393224 | tf_op jit(solution)/shard_map/ppermute | solution.py:254
  11.1 1.8 %collective-permute-done.2.early = bf16[256,640]{1,0:T(8,128)(2,1)S(1)} collective-permute-done((bf16[256,640]{1,0:T(8,128)(2,1)S(1)}, bf16[256,640]{1,0:T(8,128)(2,1)S(1)}, u32[]{:S(2)}, u32[]{:S(2)}) %collective-permute-start.2) | collective-permute-done | bytes 327712 | tf_op jit(solution)/shard_map/ppermute | solution.py:253
  12.9 0.4 %shard_map.62 = (f32[1024,256]{1,0:T(8,128)S(1)}, f32[128,256]{1,0:T(8,128)S(1)}, f32[256,256]{1,0:T(8,128)S(1)}, bf16[128,256]{1,0:T(8,128)(2,1)S(1)}, bf16[128...) custom-call(bf16[256,2048]{1,0:T(8,128)(2,1)S(1)} %copy-done, bf16[2176,256]{1,0:T(8,128)(2,1)S(1)} %get-tuple-element.30.foot, ...), custom_call_target="tpu_custom_call" | custom-call | bytes 1845000 | tf_op jit(solution)/shard_map/pallas_call | solution.py:255
  13.3 3.5 %collective-permute-done.3.fit.fit_other = bf16[256,256]{1,0:T(8,128)(2,1)S(1)} collective-permute-done((bf16[256,256]{1,0:T(8,128)(2,1)S(1)}, bf16[256,256]{1,0:T(8,128)(2,1)S(1)}, u32[]{:S(2)}, u32[]{:S(2)}) %collective-permute-start.3) | collective-permute-done | bytes 131104 | tf_op jit(solution)/shard_map/ppermute | solution.py:254
  16.8 0.6 %collective-permute-start.4 = (bf16[256,512]{1,0:T(8,128)(2,1)S(1)}, bf16[256,512]{1,0:T(8,128)(2,1)S(1)}, u32[]{:S(2)}, u32[]{:S(2)}) collective-permute-start(bf16[256,512]{1,0:T(8,128)(2,1)S(1)} %get-tuple-element.52), channel_id=1, source_target_pairs={{0,1},{1,0},{2,3},{3,2},{4,5},{5,4},{6,7},{7,6},{8,9},{9,8},{10,11... | collective-permute-start | bytes 786440 | tf_op jit(solution)/shard_map/ppermute | solution.py:271
  17.4 0.2 shard_map.66
  17.6 1.7 %collective-permute-start.5 = (bf16[128,512]{1,0:T(8,128)(2,1)S(1)}, bf16[128,512]{1,0:T(8,128)(2,1)S(1)}, u32[]{:S(2)}, u32[]{:S(2)}) collective-permute-start(bf16[128,512]{1,0:T(8,128)(2,1)S(1)} %shard_map.66), channel_id=1, source_target_pairs={{0,2},{2,4},{4,6},{6,8},{8,10},{10,12},{12,14},{14,16},{16,18},{18... | collective-permute-start | bytes 393224 | tf_op jit(solution)/shard_map/ppermute | solution.py:281
  19.4 0.6 %shard_map.63 = (f32[8,256]{1,0:T(8,128)S(1)}, bf16[256,256]{1,0:T(8,128)(2,1)S(1)}, bf16[256,256]{1,0:T(8,128)(2,1)S(1)}, f32[128,256]{1,0:T(8,128)S(1)}, f32[512,256]{1,0:T(8,128)S(1)}) custom-call(bf16[2176,256]{1,0:T(8,128)(2,1)S(1)} %get-tuple-element.30.foot, f32[1024,256]{1,0:T(8,128)S(1)} %get-tuple-element.40.total, ...), custom_call_target="tpu_custom_call" | custom-call | bytes 2952000 | tf_op jit(solution)/shard_map/pallas_call | solution.py:282
  20.0 1.2 %shard_map.64 = (bf16[1088,256]{1,0:T(8,128)(2,1)}, f32[256,256]{1,0:T(8,128)}) custom-call(bf16[2176,256]{1,0:T(8,128)(2,1)S(1)} %get-tuple-element.30.foot, f32[1024,256]{1,0:T(8,128)S(1)} %get-tuple-element.40.total, bf16[256,640]{1,0:T(8,128)(2,1)S(1)} %collective-permute-done.2.early, bf16[256,256]{1,0:T(8,128)(2,1)S(1)} %collective-permute-done.3.fit.fit_other, ...), custom_call_target="tpu_custom_call" | custom-call | bytes 4428000 | tf_op jit(solution)/shard_map/pallas_call | solution.py:295
  21.2 3.9 %collective-permute-done.4.late = bf16[256,512]{1,0:T(8,128)(2,1)S(1)} collective-permute-done((bf16[256,512]{1,0:T(8,128)(2,1)S(1)}, bf16[256,512]{1,0:T(8,128)(2,1)S(1)}, u32[]{:S(2)}, u32[]{:S(2)}) %collective-permute-start.4) | collective-permute-done | bytes 262176 | tf_op jit(solution)/shard_map/ppermute | solution.py:271
  25.1 1.0 %shard_map.65.sofar = bf16[1088,256]{1,0:T(8,128)(2,1)} custom-call(bf16[1088,256]{1,0:T(8,128)(2,1)} %get-tuple-element.50.sofar, f32[512,256]{1,0:T(8,128)S(1)} %get-tuple-element.51.waiting, bf16[256,512]{1,0:T(8,128)(2,1)S(1)} %collective-permute-done.4.late, ...), custom_call_target="tpu_custom_call", output_to_operand_aliasing={{}: (0, {})} | custom-call | bytes 3690000 | tf_op jit(solution)/shard_map/pallas_call | solution.py:303
  26.1 0.0 collective-permute-done.5.came
  26.1 0.8 %shard_map.67 = bf16[1088,256]{1,0:T(8,128)(2,1)} custom-call(bf16[1088,256]{1,0:T(8,128)(2,1)} %shard_map.65.sofar, bf16[128,512]{1,0:T(8,128)(2,1)S(1)} %collective-permute-done.5.came, bf16[256,256]{1,0:T(8,128)(2,1)S(1)} %get-tuple-element.38.fit.fit_own, ...), custom_call_target="tpu_custom_call", output_to_operand_aliasing={{}: (0, {})} | custom-call | bytes 2952000 | tf_op jit(solution)/shard_map/pallas_call | solution.py:312
Async XLA Ops:
  0.6 8.2 %copy-start = (bf16[256,2048]{1,0:T(8,128)(2,1)S(1)}, bf16[256,2048]{1,0:T(8,128)(2,1)}, u32[]{:S(2)}) copy-start(bf16[256,2048]{1,0:T(8,128)(2,1)} %movie.5) | copy-start | bytes 3145732
  0.6 8.2 %copy-start.2 = (f32[256,256]{1,0:T(8,128)S(1)}, f32[256,256]{1,0:T(8,128)}, u32[]{:S(2)}) copy-start(f32[256,256]{1,0:T(8,128)} %start.3) | copy-start | bytes 786436
  0.7 8.1 %copy-start.1 = (bf16[2176,256]{1,0:T(8,128)(2,1)S(1)}, bf16[2176,256]{1,0:T(8,128)(2,1)}, u32[]{:S(2)}) copy-start(bf16[2176,256]{1,0:T(8,128)(2,1)} %foot.3) | copy-start | bytes 3342340
  2.2 10.7 %collective-permute-start.2 = (bf16[256,640]{1,0:T(8,128)(2,1)S(1)}, bf16[256,640]{1,0:T(8,128)(2,1)S(1)}, u32[]{:S(2)}, u32[]{:S(2)}) collective-permute-start(bf16[256,640]{1,0:T(8,128)(2,1)S(1)} %get-tuple-element.39), channel_id=1, source_target_pairs={{0,1},{1,0},{2,3},{3,2},{4,5},{5,4},{6,7},{7,6},{8,9},{9,8},{10,11... | collective-permute-start | bytes 983048 | tf_op jit(solution)/shard_map/ppermute | solution.py:253
  5.2 4.8 %collective-permute-start = (bf16[256,128]{1,0:T(8,128)(2,1)S(1)}, bf16[256,128]{1,0:T(8,128)(2,1)S(1)}, u32[]{:S(2)}, u32[]{:S(2)}) collective-permute-start(bf16[256,128]{1,0:T(8,128)(2,1)S(1)} %get-tuple-element.36), channel_id=1, source_target_pairs={{2,4},{6,8},{10,12},{14,16},{18,20},{22,24},{26,28},{4,2},{8,6},{1... | collective-permute-start | bytes 196616 | tf_op jit(solution)/shard_map/ppermute | solution.py:384
  5.8 4.2 %collective-permute-start.1 = (bf16[256,128]{1,0:T(8,128)(2,1)S(1)}, bf16[256,128]{1,0:T(8,128)(2,1)S(1)}, u32[]{:S(2)}, u32[]{:S(2)}) collective-permute-start(bf16[256,128]{1,0:T(8,128)(2,1)S(1)} %get-tuple-element.37), channel_id=1, source_target_pairs={{0,2},{4,6},{8,10},{12,14},{16,18},{20,22},{24,26},{28,30},{2,0},{... | collective-permute-start | bytes 196616 | tf_op jit(solution)/shard_map/ppermute | solution.py:384
  10.5 6.4 %collective-permute-start.3 = (bf16[256,256]{1,0:T(8,128)(2,1)S(1)}, bf16[256,256]{1,0:T(8,128)(2,1)S(1)}, u32[]{:S(2)}, u32[]{:S(2)}) collective-permute-start(bf16[256,256]{1,0:T(8,128)(2,1)S(1)} %get-tuple-element.38.fit.fit_own), channel_id=1, source_target_pairs={{0,1},{1,0},{2,3},{3,2},{4,5},{5,4},{6,7},{7,6},{8,9},{9,8},{10,11... | collective-permute-start | bytes 393224 | tf_op jit(solution)/shard_map/ppermute | solution.py:254
  16.8 8.3 %collective-permute-start.4 = (bf16[256,512]{1,0:T(8,128)(2,1)S(1)}, bf16[256,512]{1,0:T(8,128)(2,1)S(1)}, u32[]{:S(2)}, u32[]{:S(2)}) collective-permute-start(bf16[256,512]{1,0:T(8,128)(2,1)S(1)} %get-tuple-element.52), channel_id=1, source_target_pairs={{0,1},{1,0},{2,3},{3,2},{4,5},{5,4},{6,7},{7,6},{8,9},{9,8},{10,11... | collective-permute-start | bytes 786440 | tf_op jit(solution)/shard_map/ppermute | solution.py:271
  17.6 8.4 %collective-permute-start.5 = (bf16[128,512]{1,0:T(8,128)(2,1)S(1)}, bf16[128,512]{1,0:T(8,128)(2,1)S(1)}, u32[]{:S(2)}, u32[]{:S(2)}) collective-permute-start(bf16[128,512]{1,0:T(8,128)(2,1)S(1)} %shard_map.66), channel_id=1, source_target_pairs={{0,2},{2,4},{4,6},{6,8},{8,10},{10,12},{12,14},{14,16},{16,18},{18... | collective-permute-start | bytes 393224 | tf_op jit(solution)/shard_map/ppermute | solution.py:281
